TPU v7x, 128 devices: a whole 4x4x4 slice. The times are simulated.
128 devices in a mesh: ctx: 8 (over x, core), ch: 16 (over y, z).
Axes of the slice: x: 4, y: 4, z: 4, core: 2. Of those that a mesh axis runs over, the one named last changes fastest.
Arguments:
- inputs: bfloat16 [2, 1024, 8192], P(None, 'ctx', 'ch'), may hold values from -6 to 6
- gates: bfloat16 [2, 1024, 8192], P(None, 'ctx', 'ch'), may hold values from -6 to 6
- conv_weight: float32 [4, 8192], P(None, 'ch'), may hold values from -3 to 3
- conv_bias: float32 [8192], P('ch'), may hold values from -3 to 3
- x_weight: bfloat16 [8192, 288], P('ch'), may hold values from -0.0625 to 0.0625
- dt_weight: bfloat16 [256, 8192], P(None, 'ch'), may hold values from -0.9375 to 0.9375
- dt_bias: float32 [8192], P('ch'), may hold values from -5 to -2
- decay_rate: float32 [16, 8192], P(None, 'ch'), may hold values from 9.765625e-06 to 1
- skip: float32 [8192], P('ch'), may hold values from 0.5 to 1.5
- lengths: int32 [2], replicated, may hold values from 256 to 1024, as said below
- row_request: int32 [512], P('ctx'), may hold values from 0 to 1
- dec_inputs: bfloat16 [4, 512, 8192], P(None, 'ctx', 'ch'), may hold values from -6 to 6
- dec_gates: bfloat16 [4, 512, 8192], P(None, 'ctx', 'ch'), may hold values from -6 to 6
Outputs:
- prefill_out: bfloat16 [2, 1024, 8192], P(None, 'ctx', 'ch')
- decode_out: bfloat16 [4, 512, 8192], P(None, 'ctx', 'ch')
Inputs may be any that keep to these rules, and one draw needn't show every extreme that they name: `lengths`: every length is at least 256, and some request has length 1024.
All inputs are finite; a program needn't handle non-finite values.
Results may differ from a plain program's by a relative error of at most 0.015.
Values may be sent and summed in bfloat16 or wider, within the bound.
A program may use at most 128 MiB of HBM per device.

v0:
```python
import functools
import math

import jax
import jax.numpy as jnp
from jax import lax
from jax.experimental import pallas as pl
from jax.experimental.pallas import tpu as pltpu
from jax.sharding import PartitionSpec as P

MESH = pl.DeviceIdType.MESH
F32 = jnp.float32
BF16 = jnp.bfloat16
LOG2E = math.log2(math.e)
KCONV = 4
SEG = 8
LANES = 128


def softplus(x):
    return jnp.maximum(x, 0.0) + jnp.log1p(jnp.exp(-jnp.abs(x)))


def silu(x):
    return x / (1.0 + jnp.exp(-x))


def row_of(value, rows=SEG):
    return jnp.broadcast_to(value, (rows, value.shape[1]))


def kernel(
    nctx, nch,
    x_ref, gate_ref, cw_ref, cb_ref, xw_ref, dtw_ref, dtb_ref, a_ref, skip_ref, len_ref, req_ref, dx_ref, dg_ref,
    out_ref, dout_ref,
    hw, xe, u_pre, u_dec, send_pre, send_dec, rs_pre, rs_dec, ag_pre, ag_dec, wx, a2, dt_pre, dt_dec, bc_pre, bc_dec,
    d_all, e_all, ssum, st32, states, hexcl, sexcl, prefix, y_pre, y_dec, mask_dec,
    hw_send, hw_recv, rsp_send, rsp_recv, rsd_send, rsd_recv, agp_send, agp_recv, agd_send, agd_recv,
    ss_send, ss_recv, st_send, st_recv,
):
    nreq, seq, width = x_ref.shape
    steps, drows = dx_ref.shape[0], dx_ref.shape[1]
    nstate = a_ref.shape[0]
    rank = dtw_ref.shape[0]
    tokens = nreq * seq
    dtokens = steps * drows
    nj = seq // SEG
    chunks = width // LANES
    nrc = nreq * chunks
    part = tokens // nch
    cols = rank + LANES
    me_ctx = lax.axis_index("ctx")
    me_ch = lax.axis_index("ch")
    offset = me_ctx * seq

    def peer(axis, me, count, k):
        return {axis: lax.rem(me + k, count)}

    barrier = pltpu.get_barrier_semaphore()
    for k in range(1, nctx):
        pl.semaphore_signal(barrier, inc=1, device_id=peer("ctx", me_ctx, nctx, k), device_id_type=MESH)
    for k in range(1, nch):
        pl.semaphore_signal(barrier, inc=1, device_id=peer("ch", me_ch, nch, k), device_id_type=MESH)

    def spread(axis, me, count, src, dst, send_sem, recv_sem):
        for k in range(1, count):
            pltpu.make_async_remote_copy(
                src_ref=src(k), dst_ref=dst(k), send_sem=send_sem, recv_sem=recv_sem,
                device_id=peer(axis, me, count, k), device_id_type=MESH,
            ).start()

    def all_of(ref, count, sem):
        view = ref.at[pl.ds(0, count - 1)]
        pltpu.make_async_copy(view, view, sem).wait()

    x2 = x_ref[...].reshape(tokens, width)
    q = lax.broadcasted_iota(jnp.int32, (16, tokens), 0)
    col = lax.broadcasted_iota(jnp.int32, (16, tokens), 1)
    win = q >= 6
    q6 = jnp.where(win, q - 6, q)
    second = q6 >= 3
    tap = jnp.where(second, q6 - 3, q6)
    length = jnp.where(second, len_ref[1], len_ref[0])
    target = jnp.where(win, length - (KCONV - 1) + tap - offset, seq - (KCONV - 1) + tap)
    good = (target >= 0) & (target < seq) & (q < 12)
    place = jnp.where(second, seq, 0) + target
    pick = jnp.where(good & (col == place), 1.0, 0.0).astype(BF16)
    hw[me_ctx] = jnp.dot(pick, x2, preferred_element_type=F32).astype(BF16)

    pl.semaphore_wait(barrier, nctx + nch - 2)
    spread("ctx", me_ctx, nctx, lambda k: hw.at[me_ctx], lambda k: hw.at[me_ctx], hw_send, hw_recv)

    i0 = lax.broadcasted_iota(jnp.int32, (seq, seq), 0)
    i1 = lax.broadcasted_iota(jnp.int32, (seq, seq), 1)
    perm = jnp.where(i1 == (i0 % SEG) * nj + i0 // SEG, 1.0, 0.0).astype(BF16)
    for r in range(nreq):
        xe[r, pl.ds(3 * SEG, seq), :] = jnp.dot(perm, x_ref[r], preferred_element_type=F32)
    k0 = lax.broadcasted_iota(jnp.int32, (2 * nstate, LANES), 0)
    k1 = lax.broadcasted_iota(jnp.int32, (2 * nstate, LANES), 1)
    twice = jnp.where((k1 == k0) | (k1 == k0 + 2 * nstate), 1.0, 0.0).astype(BF16)
    wx[:, pl.ds(0, rank)] = xw_ref[:, pl.ds(0, rank)]
    wx[:, pl.ds(rank, LANES)] = jnp.dot(
        xw_ref[:, pl.ds(rank, 2 * nstate)], twice, preferred_element_type=F32
    ).astype(BF16)
    a2[...] = a_ref[...] * (-LOG2E)
    req = jnp.broadcast_to(req_ref[...].reshape(1, drows), (drows, drows))
    d0 = lax.broadcasted_iota(jnp.int32, (drows, drows), 0)
    d1 = lax.broadcasted_iota(jnp.int32, (drows, drows), 1)
    request = jnp.sum(jnp.where((d0 == d1) & (req == 1), 1.0, 0.0), axis=1, keepdims=True)
    mask_dec[...] = jnp.broadcast_to(request, (drows, LANES))
    cb = cb_ref[...].reshape(1, width)
    dtb = dtb_ref[...].reshape(1, width)
    skip = skip_ref[...].reshape(1, width)

    lane = lax.broadcasted_iota(jnp.int32, (1, LANES), 1)
    low = lane < 2 * nstate
    high = (lane >= 2 * nstate) & (lane < 4 * nstate)

    def split(value):
        top = value.astype(BF16).astype(F32)
        return jnp.where(low, top, jnp.where(high, value - top, 0.0)).astype(BF16)

    def project(u, send):
        proj = jnp.dot(u, wx[...], preferred_element_type=F32)
        send[:, :, pl.ds(0, rank)] = proj[:, :rank].astype(BF16).reshape(nch, part, rank)
        send[:, :, pl.ds(rank, LANES)] = split(proj[:, rank:]).reshape(nch, part, LANES)

    all_of(hw, nctx, hw_recv)
    before = hw[lax.rem(me_ctx + nctx - 1, nctx)].astype(F32)
    before = jnp.where(me_ctx > 0, before, 0.0)
    sub = lax.broadcasted_iota(jnp.int32, (SEG, width), 0)
    for r in range(nreq):
        for k in range(KCONV - 1):
            last = xe[r, pl.ds((nj + k) * SEG, SEG), :]
            entry = row_of(before[3 * r + k : 3 * r + k + 1])
            xe[r, pl.ds(k * SEG, SEG), :] = jnp.where(sub == 0, entry, pltpu.roll(last, 1, 0))
        conv = cb + sum(cw_ref[k : k + 1] * xe[r, pl.ds(k * SEG, seq), :] for k in range(KCONV))
        u_pre[pl.ds(r * seq, seq), :] = silu(conv).astype(BF16).astype(F32)
    project(u_pre[...].astype(BF16), send_pre)
    spread(
        "ch", me_ch, nch, lambda k: send_pre.at[lax.rem(me_ch + k, nch)], lambda k: rs_pre.at[k - 1], rsp_send, rsp_recv
    )

    window = hw[0].astype(F32)
    for i in range(1, nctx):
        window = window + hw[i].astype(F32)
    chosen = jnp.broadcast_to(request, (drows, width)) > 0.5
    recent = [
        jnp.where(chosen, row_of(window[9 + k : 10 + k], drows), row_of(window[6 + k : 7 + k], drows))
        for k in range(KCONV - 1)
    ]
    recent = recent + [dx_ref[s].astype(F32) for s in range(steps)]
    for s in range(steps):
        conv = cb + sum(cw_ref[k : k + 1] * recent[s + k] for k in range(KCONV))
        u_dec[pl.ds(s * drows, drows), :] = silu(conv).astype(BF16).astype(F32)
    project(u_dec[...].astype(BF16), send_dec)
    spread(
        "ch", me_ch, nch, lambda k: send_dec.at[lax.rem(me_ch + k, nch)], lambda k: rs_dec.at[k - 1], rsd_send, rsd_recv
    )

    def reduce(send, rs, ag, rs_recv, ag_send, ag_recv):
        all_of(rs, nch, rs_recv)
        total = send[me_ch].astype(F32)
        for k in range(nch - 1):
            total = total + rs[k].astype(F32)
        tail = total[:, rank:]
        tail = tail + pltpu.roll(tail, 2 * nstate, 1) + pltpu.roll(tail, LANES - 2 * nstate, 1)
        ag[me_ch, :, pl.ds(0, rank)] = total[:, :rank].astype(BF16)
        ag[me_ch, :, pl.ds(rank, LANES)] = split(tail)
        spread("ch", me_ch, nch, lambda k: ag.at[me_ch], lambda k: ag.at[me_ch], ag_send, ag_recv)

    reduce(send_pre, rs_pre, ag_pre, rsp_recv, agp_send, agp_recv)
    reduce(send_dec, rs_dec, ag_dec, rsd_recv, agd_send, agd_recv)

    def expand(ag, bc):
        w0 = lax.broadcasted_iota(jnp.int32, (LANES, 2 * nstate * LANES), 0)
        w1 = lax.broadcasted_iota(jnp.int32, (LANES, 2 * nstate * LANES), 1) // LANES
        copies = jnp.where((w0 == w1) | (w0 == w1 + 2 * nstate), 1.0, 0.0).astype(BF16)
        maps = ag[:, :, pl.ds(rank, LANES)].reshape(nch * part, LANES)
        bc[...] = jnp.dot(maps, copies, preferred_element_type=F32)

    def step_sizes(ag):
        ranks = ag[:, :, pl.ds(0, rank)].reshape(nch * part, rank)
        return softplus(jnp.dot(ranks, dtw_ref[...], preferred_element_type=F32) + dtb)

    all_of(ag_pre, nch, agp_recv)
    row = lax.broadcasted_iota(jnp.int32, (seq, 1), 0)
    token = offset + (row % SEG) * nj + row // SEG
    sizes = step_sizes(ag_pre)
    for r in range(nreq):
        own = jnp.where(token < len_ref[r], sizes[r * seq : (r + 1) * seq], 0.0)
        dt_pre[pl.ds(r * seq, seq), :] = own
        whole = jnp.sum(own, axis=0, keepdims=True)
        for c in range(chunks):
            ssum[me_ctx, pl.ds(r * chunks + c, 1), :] = whole[:, c * LANES : (c + 1) * LANES]
    spread("ctx", me_ctx, nctx, lambda k: ssum.at[me_ctx], lambda k: ssum.at[me_ctx], ss_send, ss_recv)
    expand(ag_pre, bc_pre)

    sub1 = lax.broadcasted_iota(jnp.int32, (SEG, LANES), 0)

    def lanes_of(c):
        return pl.ds(pl.multiple_of(c * LANES, LANES), LANES)

    def rates(lanes):
        return [row_of(a2[n : n + 1, lanes]) for n in range(nstate)]

    def first_pass(rc, carry):
        r, c = rc // chunks, rc % chunks
        lanes = lanes_of(c)
        rate = rates(lanes)
        h = [None] * nstate
        total = None
        for j in range(nj):
            rows = pl.ds(pl.multiple_of(r * seq + j * SEG, SEG), SEG)
            dt = dt_pre[rows, lanes]
            dtu = dt * u_pre[rows, lanes]
            total = dt if j == 0 else total + dt
            for n in range(nstate):
                decay = jnp.exp2(dt * rate[n])
                d_all[rc, j, n] = decay
                drive = dtu * bc_pre[rows, n * LANES : (n + 1) * LANES]
                h[n] = drive if j == 0 else decay * h[n] + drive
        for k in (1, 2, 4):
            for n in range(nstate):
                h[n] = h[n] + jnp.exp2(rate[n] * total) * jnp.where(sub1 >= k, pltpu.roll(h[n], k, 0), 0.0)
            total = total + jnp.where(sub1 >= k, pltpu.roll(total, k, 0), 0.0)
        sexcl[rc] = jnp.where(sub1 >= 1, pltpu.roll(total, 1, 0), 0.0)
        for n in range(nstate):
            st32[rc, n : n + 1, :] = h[n][SEG - 1 :]
            hexcl[rc, n] = jnp.where(sub1 >= 1, pltpu.roll(h[n], 1, 0), 0.0)
        states[me_ctx, rc] = st32[rc].astype(BF16)
        return carry

    lax.fori_loop(0, nrc, first_pass, 0)
    spread("ctx", me_ctx, nctx, lambda k: states.at[me_ctx], lambda k: states.at[me_ctx], st_send, st_recv)

    all_of(ag_dec, nch, agd_recv)
    dt_dec[...] = step_sizes(ag_dec)
    expand(ag_dec, bc_dec)
    groups = drows // SEG

    for c in range(chunks):
        prefix[nrc, 0, c : c + 1, :] = skip[:, c * LANES : (c + 1) * LANES]

    def skip_at(c):
        return row_of(prefix[nrc, 0, pl.ds(c, 1), :])

    def decode_local(gc, carry):
        g, c = gc // chunks, gc % chunks
        lanes = lanes_of(c)
        rate = rates(lanes)
        h, product = [None] * nstate, [None] * nstate
        for s in range(steps):
            rows = pl.ds(pl.multiple_of(s * drows + g * SEG, SEG), SEG)
            dt = dt_dec[rows, lanes]
            u = u_dec[rows, lanes]
            dtu = dt * u
            y = skip_at(c) * u
            for n in range(nstate):
                decay = jnp.exp2(dt * rate[n])
                cout = bc_dec[rows, (nstate + n) * LANES : (nstate + n + 1) * LANES]
                drive = dtu * bc_dec[rows, n * LANES : (n + 1) * LANES]
                h[n] = drive if s == 0 else decay * h[n] + drive
                product[n] = decay if s == 0 else decay * product[n]
                y = y + cout * h[n]
                e_all[gc, s, n] = cout * product[n]
            y_dec[rows, lanes] = y
        return carry

    lax.fori_loop(0, groups * chunks, decode_local, 0)

    all_of(ssum, nctx, ss_recv)
    all_of(states, nctx, st_recv)

    def combine(rc, carry):
        c = rc % chunks
        rate = a2[:, lanes_of(c)]
        h = jnp.zeros((nstate, LANES), F32)
        for i in range(nctx):
            prefix[rc, i] = h
            h = jnp.exp2(rate * row_of(ssum[i, pl.ds(rc, 1), :], nstate)) * h + states[i, rc].astype(F32)
        prefix[rc, nctx] = h
        return carry

    lax.fori_loop(0, nrc, combine, 0)

    def second_pass(rc, carry):
        r, c = rc // chunks, rc % chunks
        lanes = lanes_of(c)
        rate = rates(lanes)
        start = sexcl[rc]
        h = [
            hexcl[rc, n] + jnp.exp2(rate[n] * start) * row_of(prefix[rc, me_ctx, n : n + 1, :])
            for n in range(nstate)
        ]
        for j in range(nj):
            rows = pl.ds(pl.multiple_of(r * seq + j * SEG, SEG), SEG)
            u = u_pre[rows, lanes]
            dtu = dt_pre[rows, lanes] * u
            y = skip_at(c) * u
            for n in range(nstate):
                h[n] = d_all[rc, j, n] * h[n] + dtu * bc_pre[rows, n * LANES : (n + 1) * LANES]
                y = y + bc_pre[rows, (nstate + n) * LANES : (nstate + n + 1) * LANES] * h[n]
            y_pre[rc, pl.ds(j, SEG, stride=nj), :] = y
        return carry

    lax.fori_loop(0, nrc, second_pass, 0)

    def decode_rest(gc, carry):
        g, c = gc // chunks, gc % chunks
        lanes = lanes_of(c)
        mine = mask_dec[pl.ds(pl.multiple_of(g * SEG, SEG), SEG), :] > 0.5
        h = [
            jnp.where(
                mine,
                row_of(prefix[chunks + c, nctx, n : n + 1, :]),
                row_of(prefix[c, nctx, n : n + 1, :]),
            )
            for n in range(nstate)
        ]
        for s in range(steps):
            rows = pl.ds(pl.multiple_of(s * drows + g * SEG, SEG), SEG)
            y = y_dec[rows, lanes]
            for n in range(nstate):
                y = y + e_all[gc, s, n] * h[n]
            y_dec[rows, lanes] = y
        return carry

    lax.fori_loop(0, groups * chunks, decode_rest, 0)

    natural = offset + lax.broadcasted_iota(jnp.int32, (seq, 1), 0)
    for r in range(nreq):
        live = natural < len_ref[r]
        for c in range(chunks):
            lanes = pl.ds(c * LANES, LANES)
            y = y_pre[r * chunks + c] * silu(gate_ref[r, :, lanes].astype(F32))
            out_ref[r, :, lanes] = jnp.where(live, y, 0.0).astype(BF16)
    for s in range(steps):
        dout_ref[s] = (y_dec[pl.ds(s * drows, drows), :] * silu(dg_ref[s].astype(F32))).astype(BF16)

    all_of(hw, nctx, hw_send)
    all_of(rs_pre, nch, rsp_send)
    all_of(rs_dec, nch, rsd_send)
    all_of(ag_pre, nch, agp_send)
    all_of(ag_dec, nch, agd_send)
    all_of(ssum, nctx, ss_send)
    all_of(states, nctx, st_send)


def on_device(nctx, nch, *args):
    inputs, dt_weight, decay_rate, dec_inputs = args[0], args[5], args[7], args[11]
    nreq, seq, width = inputs.shape
    steps, drows = dec_inputs.shape[:2]
    rank, nstate = dt_weight.shape[0], decay_rate.shape[0]
    tokens, dtokens = nreq * seq, steps * drows
    nj, chunks, groups = seq // SEG, width // LANES, drows // SEG
    nrc = nreq * chunks
    cols = rank + LANES
    vmem = pl.BlockSpec(memory_space=pltpu.VMEM)
    smem = pl.BlockSpec(memory_space=pltpu.SMEM)
    sem = pltpu.SemaphoreType.DMA
    scratch = [
        pltpu.VMEM((nctx, 16, width), BF16),
        pltpu.VMEM((nreq, (nj + KCONV - 1) * SEG, width), F32),
        pltpu.VMEM((tokens, width), F32),
        pltpu.VMEM((dtokens, width), F32),
        pltpu.VMEM((nch, tokens // nch, cols), BF16),
        pltpu.VMEM((nch, dtokens // nch, cols), BF16),
        pltpu.VMEM((nch - 1, tokens // nch, cols), BF16),
        pltpu.VMEM((nch - 1, dtokens // nch, cols), BF16),
        pltpu.VMEM((nch, tokens // nch, cols), BF16),
        pltpu.VMEM((nch, dtokens // nch, cols), BF16),
        pltpu.VMEM((width, cols), BF16),
        pltpu.VMEM((nstate, width), F32),
        pltpu.VMEM((tokens, width), F32),
        pltpu.VMEM((dtokens, width), F32),
        pltpu.VMEM((tokens, 2 * nstate * LANES), F32),
        pltpu.VMEM((dtokens, 2 * nstate * LANES), F32),
        pltpu.VMEM((nrc, nj, nstate, SEG, LANES), F32),
        pltpu.VMEM((groups * chunks, steps, nstate, SEG, LANES), F32),
        pltpu.VMEM((nctx, nrc, LANES), F32),
        pltpu.VMEM((nrc, nstate, LANES), F32),
        pltpu.VMEM((nctx, nrc, nstate, LANES), BF16),
        pltpu.VMEM((nrc, nstate, SEG, LANES), F32),
        pltpu.VMEM((nrc, SEG, LANES), F32),
        pltpu.VMEM((nrc + 1, nctx + 1, nstate, LANES), F32),
        pltpu.VMEM((nrc, seq, LANES), F32),
        pltpu.VMEM((dtokens, width), F32),
        pltpu.VMEM((drows, LANES), F32),
    ] + [sem] * 14
    return pl.pallas_call(
        functools.partial(kernel, nctx, nch),
        out_shape=(
            jax.ShapeDtypeStruct(inputs.shape, BF16),
            jax.ShapeDtypeStruct(dec_inputs.shape, BF16),
        ),
        in_specs=[vmem] * 9 + [smem] + [vmem] * 3,
        out_specs=(vmem, vmem),
        scratch_shapes=scratch,
        compiler_params=pltpu.CompilerParams(
            collective_id=0, has_side_effects=True, vmem_limit_bytes=56 * 1024 * 1024
        ),
    )(*args)


def solution(mesh):
    placed = (
        P(None, "ctx", "ch"),
        P(None, "ctx", "ch"),
        P(None, "ch"),
        P("ch"),
        P("ch", None),
        P(None, "ch"),
        P("ch"),
        P(None, "ch"),
        P("ch"),
        P(),
        P("ctx"),
        P(None, "ctx", "ch"),
        P(None, "ctx", "ch"),
    )
    return jax.shard_map(
        functools.partial(on_device, mesh.shape["ctx"], mesh.shape["ch"]),
        mesh=mesh,
        in_specs=placed,
        out_specs=(P(None, "ctx", "ch"), P(None, "ctx", "ch")),
        check_vma=False,
    )
```

profile of v0, /device:TPU:1, one launch (start us, length us, event | category | flops | bytes accessed | tf_op | source)
XLA Modules:
  0.0 44.7 jit_solution(8644738751008535548)
XLA Ops:
  0.6 1.9 %copy.15.xw_ref = bf16[512,288]{1,0:T(8,128)(2,1)} copy(bf16[512,288]{0,1:T(8,128)(2,1)} %param.17) | data formatting | bytes 589824 | tf_op args[4]
  2.5 39.8 %shard_map.140 = (bf16[2,128,512]{2,1,0:T(8,128)(2,1)}, bf16[4,64,512]{2,1,0:T(8,128)(2,1)}) custom-call(bf16[2,128,512]{2,1,0:T(8,128)(2,1)} %x_ref.1, bf16[2,128,512]{2,1,0:T(8,128)(2,1)} %gate_ref.1, f32[4,512]{1,0:T(4,128)} %cw_ref.1, f32[512]{0:T(512)} %cb_ref.1, bf16[512,288]{1,0:T(8,128)(2,1)} %copy.15.xw_ref, bf16[256,512]{1,0:T(8,128)(2,1)} %dtw_ref.1, ...), custom_call_target="tpu_custom_call" | custom-call | tf_op jit(solution)/shard_map/pallas_call | solution.py:391
  42.3 0.0 copy-start
  42.3 1.7 %copy.18 = bf16[2,128,512]{2,1,0:T(8,128)(2,1)} copy(bf16[2,128,512]{2,1,0:T(8,128)(2,1)} %get-tuple-element.4) | data formatting | bytes 524288
  44.0 0.0 copy-done
  44.0 0.7 %copy.19 = bf16[4,64,512]{2,1,0:T(8,128)(2,1)} copy(bf16[4,64,512]{2,1,0:T(8,128)(2,1)S(1)} %copy-done) | data formatting | bytes 524288
Async XLA Ops:
  42.3 1.7 %copy-start = (bf16[4,64,512]{2,1,0:T(8,128)(2,1)S(1)}, bf16[4,64,512]{2,1,0:T(8,128)(2,1)}, u32[]{:S(2)}) copy-start(bf16[4,64,512]{2,1,0:T(8,128)(2,1)} %get-tuple-element.5) | copy-start | bytes 786436
where the time goes:
time: 44.9 us; the launch traced here: 44.7 us
  Pallas kernels  39.8 us (89%)
  local copies, waits for them, and re-layouts  4.3 us (10%)
  between operations  0.65 us (1%)
    pallas_call x1, Pallas kernels, on_device(): pl.pallas_call(functools.partial(kernel, nctx, nch), out_shape=(jax.Shape...  39.8 us
    unnamed x5, local copies, waits for them, and re-layouts  4.3 us

commit v1 on v0

v1 whole, which is shorter than its diff:
```python
import functools
import math

import jax
import jax.numpy as jnp
from jax import lax
from jax.experimental import pallas as pl
from jax.experimental.pallas import tpu as pltpu
from jax.sharding import PartitionSpec as P

MESH = pl.DeviceIdType.MESH
F32 = jnp.float32
BF16 = jnp.bfloat16
LOG2E = math.log2(math.e)
KCONV = 4
SEG = 8
LANES = 128
SIDE = 4


def softplus(x):
    return jnp.maximum(x, 0.0) + jnp.log1p(jnp.exp(-jnp.abs(x)))


def silu(x):
    return x / (1.0 + jnp.exp(-x))


def row_of(value, rows=SEG):
    return jnp.broadcast_to(value, (rows, value.shape[1]))


def total_of(terms):
    while len(terms) > 1:
        terms = [a + b for a, b in zip(terms[::2], terms[1::2])] + ([terms[-1]] if len(terms) % 2 else [])
    return terms[0]


def ring(d):
    return min(d, SIDE - d)


def kernel(
    nctx, nch,
    x_hbm, gate_hbm, cw_hbm, cb_hbm, xw_hbm, dtw_hbm, dtb_hbm, a_hbm, skip_hbm, len_ref, req_hbm, dx_hbm, dg_hbm,
    out_ref, dout_ref,
    x_ref, gate_ref, cw_ref, cb_ref, xw_ref, dtw_ref, dtb_ref, a_ref, skip_ref, req_ref, dx_ref, dg_ref,
    hw, xe, u_pre, u_dec, edge_u, edge, send_pre, send_dec, rs_pre, rs_dec, ag_pre, ag_dec, wx, a2, skips,
    dt_pre, dt_dec, bc_pre, bc_dec, d_all, e_pre, e_dec, ssum, st32, states, hexcl, sexcl, pseg, weight, prefix,
    y_loc, y_nat, y_dec, y_half, y_fin, g_pre, g_dec, mask_dec,
    in_sems, hw_send, hw_recv, ed_send, ed_recv, rsp_send, rsp_recv, rsd_send, rsd_recv,
    agp_send, agp_recv, agd_send, agd_recv, ss_send, ss_recv, st_send, st_recv,
):
    nreq, seq, width = x_ref.shape
    steps, drows = dx_ref.shape[0], dx_ref.shape[1]
    nstate = a_ref.shape[0]
    rank = dtw_ref.shape[0]
    tokens = nreq * seq
    nj = seq // SEG
    chunks = width // LANES
    nrc = nreq * chunks
    groups = drows // SEG
    part = tokens // nch
    me_ctx = lax.axis_index("ctx")
    me_ch = lax.axis_index("ch")
    offset = me_ctx * seq

    pairs = [
        (x_hbm, x_ref), (xw_hbm, xw_ref), (cw_hbm, cw_ref), (cb_hbm, cb_ref), (dx_hbm, dx_ref), (req_hbm, req_ref),
        (dtw_hbm, dtw_ref), (dtb_hbm, dtb_ref), (a_hbm, a_ref), (skip_hbm, skip_ref), (gate_hbm, gate_ref),
        (dg_hbm, dg_ref),
    ]
    loads = []
    for i, (src, dst) in enumerate(pairs):
        if dst.dtype == BF16 and len(dst.shape) == 3:
            pieces = [(k, pl.ds(j * 32, 32)) for k in range(dst.shape[0]) for j in range(dst.shape[1] // 32)]
        elif dst.dtype == BF16:
            pieces = [(pl.ds(j * 32, 32),) for j in range(dst.shape[0] // 32)]
        else:
            pieces = [None]
        sem = in_sems.at[i]
        for piece in pieces:
            if piece is None:
                pltpu.make_async_copy(src, dst, sem).start()
            else:
                pltpu.make_async_copy(src.at[piece], dst.at[piece], sem).start()
        loads.append(pltpu.make_async_copy(src, dst, sem))

    def far_ch():
        for k in sorted(range(1, nch), key=lambda k: -(ring(k // SIDE) + ring(k % SIDE))):
            y = lax.rem(me_ch // SIDE + k // SIDE, nch // SIDE)
            z = lax.rem(lax.rem(me_ch, SIDE) + k % SIDE, SIDE)
            yield k, y * SIDE + z

    def far_ctx():
        for k in sorted(range(1, nctx), key=lambda k: -ring(k // 2)):
            x = lax.rem(me_ctx // 2 + k // 2, nctx // 2)
            core = lax.rem(lax.rem(me_ctx, 2) + k % 2, 2)
            yield k, x * 2 + core

    far = {"ch": far_ch, "ctx": far_ctx}

    barrier = pltpu.get_barrier_semaphore()
    for axis in ("ch", "ctx"):
        for k, to in far[axis]():
            pl.semaphore_signal(barrier, inc=1, device_id={axis: to}, device_id_type=MESH)

    def spread(axis, src, dst, send_sem, recv_sem):
        for k, to in far[axis]():
            pltpu.make_async_remote_copy(
                src_ref=src(to), dst_ref=dst(k), send_sem=send_sem, recv_sem=recv_sem,
                device_id={axis: to}, device_id_type=MESH,
            ).start()

    def all_of(ref, count, sem):
        view = ref.at[pl.ds(0, count - 1)]
        pltpu.make_async_copy(view, view, sem).wait()

    i0 = lax.broadcasted_iota(jnp.int32, (seq, seq), 0)
    i1 = lax.broadcasted_iota(jnp.int32, (seq, seq), 1)
    perm = jnp.where(i1 == (i0 % SEG) * nj + i0 // SEG, 1.0, 0.0).astype(BF16)
    lane = lax.broadcasted_iota(jnp.int32, (1, LANES), 1)
    low = lane < 2 * nstate
    high = (lane >= 2 * nstate) & (lane < 4 * nstate)

    def split(value):
        top = value.astype(BF16).astype(F32)
        return jnp.where(low, top, jnp.where(high, value - top, 0.0)).astype(BF16)

    def project(u):
        return lax.dot_general(u, wx[...], (((1,), (1,)), ((), ())), preferred_element_type=F32)

    def fill(send, proj):
        send[:, :, pl.ds(0, rank)] = proj[:, :rank].astype(BF16).reshape(nch, part, rank)
        send[:, :, pl.ds(rank, LANES)] = split(proj[:, rank:]).reshape(nch, part, LANES)

    loads[0].wait()
    x2 = x_ref[...].reshape(tokens, width)
    q = lax.broadcasted_iota(jnp.int32, (16, tokens), 0)
    col = lax.broadcasted_iota(jnp.int32, (16, tokens), 1)
    win = q >= 6
    q6 = jnp.where(win, q - 6, q)
    second = q6 >= 3
    tap = jnp.where(second, q6 - 3, q6)
    length = jnp.where(second, len_ref[1], len_ref[0])
    target = jnp.where(win, length - (KCONV - 1) + tap - offset, seq - (KCONV - 1) + tap)
    good = (target >= 0) & (target < seq) & (q < 12)
    place = jnp.where(second, seq, 0) + target
    pick = jnp.where(good & (col == place), 1.0, 0.0).astype(BF16)
    hw[me_ctx] = jnp.dot(pick, x2, preferred_element_type=F32).astype(BF16)
    pl.semaphore_wait(barrier, nctx + nch - 2)
    spread("ctx", lambda to: hw.at[me_ctx], lambda k: hw.at[me_ctx], hw_send, hw_recv)

    sub = lax.broadcasted_iota(jnp.int32, (SEG, width), 0)
    for r in range(nreq):
        xe[r, pl.ds(3 * SEG, seq), :] = jnp.dot(perm, x_ref[r], preferred_element_type=F32)
    loads[1].wait()
    wx[pl.ds(0, rank + 2 * nstate), :] = xw_ref[...]
    wx[pl.ds(rank + 2 * nstate, 2 * nstate), :] = xw_ref[pl.ds(rank, 2 * nstate), :]
    wx[pl.ds(rank + 4 * nstate, LANES - 4 * nstate), :] = jnp.zeros((LANES - 4 * nstate, width), BF16)
    loads[2].wait()
    loads[3].wait()
    cb = cb_ref[...].reshape(1, width)
    for r in range(nreq):
        for k in range(KCONV - 1):
            last = xe[r, pl.ds((nj + k) * SEG, SEG), :]
            xe[r, pl.ds(k * SEG, SEG), :] = jnp.where(sub == 0, 0.0, pltpu.roll(last, 1, 0))
        conv = cb + sum(cw_ref[k : k + 1] * xe[r, pl.ds(k * SEG, seq), :] for k in range(KCONV))
        u_pre[pl.ds(r * seq, seq), :] = silu(conv).astype(BF16).astype(F32)
    fill(send_pre, project(u_pre[...].astype(BF16)))
    spread("ch", lambda to: send_pre.at[to], lambda k: rs_pre.at[k - 1], rsp_send, rsp_recv)

    for load in loads[4:10]:
        load.wait()
    a2[...] = a_ref[...] * (-LOG2E)
    dtb = dtb_ref[...].reshape(1, width)
    skip = skip_ref[...].reshape(1, width)
    for c in range(chunks):
        skips[c : c + 1, :] = skip[:, c * LANES : (c + 1) * LANES]
    req = jnp.broadcast_to(req_ref[...].reshape(1, drows), (drows, drows))
    d0 = lax.broadcasted_iota(jnp.int32, (drows, drows), 0)
    d1 = lax.broadcasted_iota(jnp.int32, (drows, drows), 1)
    request = jnp.sum(jnp.where((d0 == d1) & (req == 1), 1.0, 0.0), axis=1, keepdims=True)
    mask_dec[...] = jnp.broadcast_to(request, (drows, LANES))
    edge_u[...] = jnp.zeros_like(edge_u)

    all_of(hw, nctx, hw_recv)
    before = hw[lax.rem(me_ctx + nctx - 1, nctx)].astype(F32)
    before = jnp.where(me_ctx > 0, before, 0.0)
    edges = KCONV - 1
    for r in range(nreq):
        for k in range(edges):
            own = xe[r, pl.ds(k * SEG, SEG), :]
            xe[r, pl.ds(k * SEG, SEG), :] = jnp.where(sub == 0, row_of(before[3 * r + k : 3 * r + k + 1]), own)
        conv = cb + sum(cw_ref[k : k + 1] * xe[r, pl.ds(k * SEG, edges * SEG), :] for k in range(KCONV))
        u = silu(conv).astype(BF16).astype(F32)
        u_pre[pl.ds(r * seq, edges * SEG), :] = u
        for k in range(edges):
            edge_u[edges * r + k : edges * r + k + 1, :] = u[k * SEG : k * SEG + 1]
    edge_proj = project(edge_u[...].astype(BF16))
    spot = lax.broadcasted_iota(jnp.int32, (16, LANES), 0)
    left = lax.broadcasted_iota(jnp.int32, (16, LANES), 1)
    count = nreq * edges
    maps = jnp.where(left < 2 * nstate, edge_proj[:, rank:], 0.0)
    packed = jnp.where(spot >= 2 * count, pltpu.roll(maps, 2 * count, 0), 0.0)
    wrapped = pltpu.roll(pltpu.roll(maps, 2 * count - 4, 0), 2 * nstate, 1)
    packed = packed + jnp.where((spot >= 2 * count) & (spot < 3 * count - 4), wrapped, 0.0)
    packed = packed + pltpu.roll(packed, LANES // 2, 1)
    coarse = packed.astype(BF16).astype(F32)
    packed = jnp.where(left < LANES // 2, coarse, packed - coarse)
    lower = pltpu.roll(edge_proj[:, LANES:rank], count, 0)
    packed = jnp.where(spot < count, edge_proj[:, :LANES], jnp.where(spot < 2 * count, lower, packed))
    edge[me_ch] = packed.astype(BF16)
    spread("ch", lambda to: edge.at[me_ch], lambda k: edge.at[me_ch], ed_send, ed_recv)

    window = total_of([hw[i].astype(F32) for i in range(nctx)])
    chosen = jnp.broadcast_to(request, (drows, width)) > 0.5
    recent = [
        jnp.where(chosen, row_of(window[9 + k : 10 + k], drows), row_of(window[6 + k : 7 + k], drows))
        for k in range(KCONV - 1)
    ]
    recent = recent + [dx_ref[s].astype(F32) for s in range(steps)]
    for s in range(steps):
        conv = cb + sum(cw_ref[k : k + 1] * recent[s + k] for k in range(KCONV))
        u_dec[pl.ds(s * drows, drows), :] = silu(conv).astype(BF16).astype(F32)
    fill(send_dec, project(u_dec[...].astype(BF16)))
    spread("ch", lambda to: send_dec.at[to], lambda k: rs_dec.at[k - 1], rsd_send, rsd_recv)

    def summed(terms):
        total = total_of(terms)
        tail = total[:, rank:]
        tail = tail + pltpu.roll(tail, 2 * nstate, 1) + pltpu.roll(tail, LANES - 2 * nstate, 1)
        return total[:, :rank].astype(BF16), split(tail)

    def reduce(send, rs, ag, rs_recv, ag_send, ag_recv):
        all_of(rs, nch, rs_recv)
        head, tail = summed([send[me_ch].astype(F32)] + [rs[k].astype(F32) for k in range(nch - 1)])
        ag[me_ch, :, pl.ds(0, rank)] = head
        ag[me_ch, :, pl.ds(rank, LANES)] = tail
        spread("ch", lambda to: ag.at[me_ch], lambda k: ag.at[me_ch], ag_send, ag_recv)

    reduce(send_pre, rs_pre, ag_pre, rsp_recv, agp_send, agp_recv)
    for load in loads[10:]:
        load.wait()
    for r in range(nreq):
        for c in range(chunks):
            g_pre[r * chunks + c] = silu(gate_ref[r, :, c * LANES : (c + 1) * LANES].astype(F32))
    for s in range(steps):
        g_dec[pl.ds(s * drows, drows), :] = silu(dg_ref[s].astype(F32))
    reduce(send_dec, rs_dec, ag_dec, rsd_recv, agd_send, agd_recv)

    w0 = lax.broadcasted_iota(jnp.int32, (LANES, 2 * nstate * LANES), 0)
    w1 = lax.broadcasted_iota(jnp.int32, (LANES, 2 * nstate * LANES), 1) // LANES
    copies = jnp.where((w0 == w1) | (w0 == w1 + 2 * nstate), 1.0, 0.0).astype(BF16)

    def expand(proj, bc, ats):
        for at in ats:
            half = pl.ds(at * nstate * LANES, nstate * LANES)
            own = copies[:, at * nstate * LANES : (at + 1) * nstate * LANES]
            bc[:, half] = jnp.dot(proj[:, rank:], own, preferred_element_type=F32)

    def step_sizes(proj):
        return softplus(jnp.dot(proj[:, :rank], dtw_ref[...], preferred_element_type=F32) + dtb)

    all_of(edge, nch, ed_recv)
    whole = total_of([edge[i].astype(F32) for i in range(nch)])
    maps = whole + pltpu.roll(whole, LANES // 2, 1)
    spread_maps = pltpu.roll(maps, 16 - 2 * count, 0)
    wrapped = pltpu.roll(pltpu.roll(maps, 16 - 2 * count + 4, 0), LANES - 2 * nstate, 1)
    maps = jnp.where(spot < 4, spread_maps, wrapped)
    maps = jnp.where(left < 2 * nstate, maps, pltpu.roll(maps, 2 * nstate, 1))
    fixed = jnp.concatenate(
        [
            whole.astype(BF16).astype(F32),
            pltpu.roll(whole, 16 - count, 0).astype(BF16).astype(F32),
            split(maps).astype(F32),
        ],
        axis=1,
    )
    all_of(ag_pre, nch, agp_recv)
    which = lax.broadcasted_iota(jnp.int32, (part, rank + LANES), 0)
    blocks = []
    for p in range(nch):
        block = ag_pre[p]
        spots = [
            (edges * r + k, r * seq + k * SEG - p * part)
            for r in range(nreq)
            for k in range(edges)
            if 0 <= r * seq + k * SEG - p * part < part
        ]
        for at, spot in spots:
            block = jnp.where(which == spot, row_of(fixed[at : at + 1], part), block.astype(F32)).astype(BF16)
        blocks.append(block)
    proj_pre = jnp.concatenate(blocks, axis=0)

    row = lax.broadcasted_iota(jnp.int32, (seq, 1), 0)
    token = offset + (row % SEG) * nj + row // SEG
    sizes = step_sizes(proj_pre)
    for r in range(nreq):
        own = jnp.where(token < len_ref[r], sizes[r * seq : (r + 1) * seq], 0.0)
        dt_pre[pl.ds(r * seq, seq), :] = own
        whole = jnp.sum(own, axis=0, keepdims=True)
        for c in range(chunks):
            ssum[me_ctx, pl.ds(r * chunks + c, 1), :] = whole[:, c * LANES : (c + 1) * LANES]
    spread("ctx", lambda to: ssum.at[me_ctx], lambda k: ssum.at[me_ctx], ss_send, ss_recv)
    expand(proj_pre, bc_pre, (0,))

    sub1 = lax.broadcasted_iota(jnp.int32, (SEG, LANES), 0)

    def lanes_of(c):
        return pl.ds(pl.multiple_of(c * LANES, LANES), LANES)

    def rates(lanes):
        return [row_of(a2[n : n + 1, lanes]) for n in range(nstate)]

    def of(n):
        return pl.ds(n * LANES, LANES)

    def first_pass(r):
        def body(c, carry):
            rc = r * chunks + c
            lanes = lanes_of(c)
            rate = rates(lanes)
            h = [None] * nstate
            total = None
            for j in range(nj):
                rows = pl.ds(r * seq + j * SEG, SEG)
                dt = dt_pre[rows, lanes]
                dtu = dt * u_pre[rows, lanes]
                total = dt if j == 0 else total + dt
                for n in range(nstate):
                    decay = jnp.exp2(dt * rate[n])
                    d_all[rc, j, n] = decay
                    drive = dtu * bc_pre[rows, of(n)]
                    h[n] = drive if j == 0 else decay * h[n] + drive
            for k in (1, 2, 4):
                for n in range(nstate):
                    h[n] = h[n] + jnp.exp2(rate[n] * total) * jnp.where(sub1 >= k, pltpu.roll(h[n], k, 0), 0.0)
                total = total + jnp.where(sub1 >= k, pltpu.roll(total, k, 0), 0.0)
            for n in range(nstate):
                st32[rc, n : n + 1, :] = h[n][SEG - 1 :]
            states[r, me_ctx, c] = st32[rc].astype(BF16)
            sexcl[rc] = jnp.where(sub1 >= 1, pltpu.roll(total, 1, 0), 0.0)
            for n in range(nstate):
                hexcl[rc, n] = jnp.where(sub1 >= 1, pltpu.roll(h[n], 1, 0), 0.0)
            return carry

        lax.fori_loop(0, chunks, body, 0)
        spread(
            "ctx", lambda to: states.at[r, me_ctx], lambda k: states.at[r, me_ctx], st_send.at[r], st_recv.at[r]
        )

    for r in range(nreq):
        first_pass(r)

    expand(proj_pre, bc_pre, (1,))

    all_of(ag_dec, nch, agd_recv)
    proj_dec = ag_dec[...].reshape(nch * part, rank + LANES)
    dt_dec[...] = step_sizes(proj_dec)
    expand(proj_dec, bc_dec, (0, 1))

    def decode_local(gc, carry):
        g, c = gc // chunks, gc % chunks
        lanes = lanes_of(c)
        rate = rates(lanes)
        skipping = row_of(skips[pl.ds(c, 1), :])
        h, product = [None] * nstate, [None] * nstate
        for s in range(steps):
            rows = pl.ds(pl.multiple_of(s * drows + g * SEG, SEG), SEG)
            dt = dt_dec[rows, lanes]
            u = u_dec[rows, lanes]
            dtu = dt * u
            terms = [skipping * u]
            for n in range(nstate):
                decay = jnp.exp2(dt * rate[n])
                cout = bc_dec[rows, of(nstate + n)]
                drive = dtu * bc_dec[rows, of(n)]
                h[n] = drive if s == 0 else decay * h[n] + drive
                product[n] = decay if s == 0 else decay * product[n]
                terms.append(cout * h[n])
                e_dec[gc, s, n] = cout * product[n]
            y_dec[rows, lanes] = total_of(terms)
        return carry

    lax.fori_loop(0, groups * chunks, decode_local, 0)

    def prefill_local(rc, carry):
        r, c = rc // chunks, rc % chunks
        lanes = lanes_of(c)
        skipping = row_of(skips[pl.ds(c, 1), :])
        h = [hexcl[rc, n] for n in range(nstate)]
        for n in range(nstate):
            pseg[rc, n] = jnp.exp2(row_of(a2[n : n + 1, lanes]) * sexcl[rc])
        product = [None] * nstate
        for j in range(nj):
            rows = pl.ds(pl.multiple_of(r * seq + j * SEG, SEG), SEG)
            u = u_pre[rows, lanes]
            dtu = dt_pre[rows, lanes] * u
            terms = [skipping * u]
            for n in range(nstate):
                decay = d_all[rc, j, n]
                cout = bc_pre[rows, of(nstate + n)]
                h[n] = decay * h[n] + dtu * bc_pre[rows, of(n)]
                product[n] = decay if j == 0 else decay * product[n]
                terms.append(cout * h[n])
                e_pre[rc, j, n] = cout * product[n]
            y_loc[rc, j] = total_of(terms)
        return carry

    lax.fori_loop(0, nrc, prefill_local, 0)

    all_of(ssum, nctx, ss_recv)
    for rc in range(nrc):
        rate = a2[:, (rc % chunks) * LANES : (rc % chunks + 1) * LANES]
        for i in range(nctx):
            weight[rc, i] = jnp.exp2(rate * row_of(ssum[i, rc : rc + 1, :], nstate))

    for r in range(nreq):
        all_of(states.at[r], nctx, st_recv.at[r])
        for c in range(chunks):
            rc = r * chunks + c
            h = jnp.zeros((nstate, LANES), F32)
            for i in range(nctx):
                prefix[rc, i] = h
                h = weight[rc, i] * h + states[r, i, c].astype(F32)
            prefix[rc, nctx] = h

    def prefill_rest(rc, carry):
        h = [pseg[rc, n] * row_of(prefix[rc, me_ctx, n : n + 1, :]) for n in range(nstate)]
        for j in range(nj):
            y = total_of([y_loc[rc, j]] + [e_pre[rc, j, n] * h[n] for n in range(nstate)])
            y_nat[rc, pl.ds(j, SEG, stride=nj), :] = y
        return carry

    lax.fori_loop(0, nrc, prefill_rest, 0)

    def decode_rest(c, carry):
        lanes = lanes_of(c)
        half = nstate // 2
        for first in (0, half):
            at = range(first, first + half)
            f0 = [row_of(prefix[c, nctx, n : n + 1, :]) for n in at]
            f1 = [row_of(prefix[chunks + c, nctx, n : n + 1, :]) for n in at]
            for g in range(groups):
                mine = mask_dec[g * SEG : (g + 1) * SEG, :] > 0.5
                h = [jnp.where(mine, b, a) for a, b in zip(f0, f1)]
                for s in range(steps):
                    rows = pl.ds(s * drows + g * SEG, SEG)
                    terms = [e_dec[g * chunks + c, s, n] * h[n - first] for n in at]
                    if first == 0:
                        y_half[rows, lanes] = total_of(terms + [y_dec[rows, lanes]])
                    else:
                        y_fin[rows, lanes] = total_of(terms + [y_half[rows, lanes]]) * g_dec[rows, lanes]
        return carry

    lax.fori_loop(0, chunks, decode_rest, 0)

    natural = offset + lax.broadcasted_iota(jnp.int32, (seq, 1), 0)
    for r in range(nreq):
        live = natural < len_ref[r]
        for c in range(chunks):
            y = y_nat[r * chunks + c] * g_pre[r * chunks + c]
            out_ref[r, :, pl.ds(c * LANES, LANES)] = jnp.where(live, y, 0.0).astype(BF16)
    for s in range(steps):
        dout_ref[s] = y_fin[pl.ds(s * drows, drows), :].astype(BF16)

    all_of(hw, nctx, hw_send)
    all_of(edge, nch, ed_send)
    all_of(rs_pre, nch, rsp_send)
    all_of(rs_dec, nch, rsd_send)
    all_of(ag_pre, nch, agp_send)
    all_of(ag_dec, nch, agd_send)
    all_of(ssum, nctx, ss_send)
    for r in range(nreq):
        all_of(states.at[r], nctx, st_send.at[r])


def on_device(nctx, nch, *args):
    args = list(args)
    args[4] = args[4].T
    inputs, dt_weight, decay_rate, row_request, dec_inputs = args[0], args[5], args[7], args[10], args[11]
    nreq, seq, width = inputs.shape
    steps, drows = dec_inputs.shape[:2]
    rank, nstate = dt_weight.shape[0], decay_rate.shape[0]
    tokens, dtokens = nreq * seq, steps * drows
    nj, chunks, groups = seq // SEG, width // LANES, drows // SEG
    nrc = nreq * chunks
    cols = rank + LANES
    part, dpart = tokens // nch, dtokens // nch
    hbm = pl.BlockSpec(memory_space=pl.ANY)
    vmem = pl.BlockSpec(memory_space=pltpu.VMEM)
    smem = pl.BlockSpec(memory_space=pltpu.SMEM)
    sem = pltpu.SemaphoreType.DMA
    scratch = [pltpu.VMEM(a.shape, a.dtype) for i, a in enumerate(args) if i != 9] + [
        pltpu.VMEM((nctx, 16, width), BF16),
        pltpu.VMEM((nreq, (nj + KCONV - 1) * SEG, width), F32),
        pltpu.VMEM((tokens, width), F32),
        pltpu.VMEM((dtokens, width), F32),
        pltpu.VMEM((16, width), F32),
        pltpu.VMEM((nch, 16, LANES), BF16),
        pltpu.VMEM((nch, part, cols), BF16),
        pltpu.VMEM((nch, dpart, cols), BF16),
        pltpu.VMEM((nch - 1, part, cols), BF16),
        pltpu.VMEM((nch - 1, dpart, cols), BF16),
        pltpu.VMEM((nch, part, cols), BF16),
        pltpu.VMEM((nch, dpart, cols), BF16),
        pltpu.VMEM((cols, width), BF16),
        pltpu.VMEM((nstate, width), F32),
        pltpu.VMEM((8, LANES), F32),
        pltpu.VMEM((tokens, width), F32),
        pltpu.VMEM((dtokens, width), F32),
        pltpu.VMEM((tokens, 2 * nstate * LANES), F32),
        pltpu.VMEM((dtokens, 2 * nstate * LANES), F32),
        pltpu.VMEM((nrc, nj, nstate, SEG, LANES), F32),
        pltpu.VMEM((nrc, nj, nstate, SEG, LANES), F32),
        pltpu.VMEM((groups * chunks, steps, nstate, SEG, LANES), F32),
        pltpu.VMEM((nctx, nrc, LANES), F32),
        pltpu.VMEM((nrc, nstate, LANES), F32),
        pltpu.VMEM((nreq, nctx, chunks, nstate, LANES), BF16),
        pltpu.VMEM((nrc, nstate, SEG, LANES), F32),
        pltpu.VMEM((nrc, SEG, LANES), F32),
        pltpu.VMEM((nrc, nstate, SEG, LANES), F32),
        pltpu.VMEM((nrc, nctx, nstate, LANES), F32),
        pltpu.VMEM((nrc, nctx + 1, nstate, LANES), F32),
        pltpu.VMEM((nrc, nj, SEG, LANES), F32),
        pltpu.VMEM((nrc, seq, LANES), F32),
        pltpu.VMEM((dtokens, width), F32),
        pltpu.VMEM((dtokens, width), F32),
        pltpu.VMEM((dtokens, width), F32),
        pltpu.VMEM((nrc, seq, LANES), F32),
        pltpu.VMEM((dtokens, width), F32),
        pltpu.VMEM((drows, LANES), F32),
        sem((len(args) - 1,)),
    ] + [sem] * 14 + [sem((nreq,))] * 2
    shapes = (jax.ShapeDtypeStruct(inputs.shape, BF16), jax.ShapeDtypeStruct(dec_inputs.shape, BF16))
    return pl.pallas_call(
        functools.partial(kernel, nctx, nch),
        out_shape=tuple(pltpu.VMEM(s.shape, s.dtype) for s in shapes),
        in_specs=[hbm] * 9 + [smem] + [hbm] * 3,
        out_specs=(vmem, vmem),
        scratch_shapes=scratch,
        compiler_params=pltpu.CompilerParams(
            collective_id=0, has_side_effects=True, vmem_limit_bytes=65011712 + 1536 * 1024 - 64 * 1024
        ),
    )(*args)


def solution(mesh):
    placed = (
        P(None, "ctx", "ch"),
        P(None, "ctx", "ch"),
        P(None, "ch"),
        P("ch"),
        P("ch", None),
        P(None, "ch"),
        P("ch"),
        P(None, "ch"),
        P("ch"),
        P(),
        P("ctx"),
        P(None, "ctx", "ch"),
        P(None, "ctx", "ch"),
    )
    return jax.shard_map(
        functools.partial(on_device, mesh.shape["ctx"], mesh.shape["ch"]),
        mesh=mesh,
        in_specs=placed,
        out_specs=(P(None, "ctx", "ch"), P(None, "ctx", "ch")),
        check_vma=False,
    )
```

time: 44.9 us -> 34.4 us (0.77)
  Pallas kernels: 39.8 us -> 32.2 us
  local copies, waits for them, and re-layouts: 4.3 us -> 1.41 us
    pallas_call x1, Pallas kernels: 39.8 us -> 32.2 us  [on_device(): pl.pallas_call(functools.partial(kernel, nctx, nch), out_shape=tuple((plt...]
    unnamed x5 -> x2, local copies, waits for them, and re-layouts: 4.3 us -> 1.41 us
where the time goes in v1:
time: 34.4 us; the launch traced here: 34.2 us
  Pallas kernels  32.2 us (94%)
  local copies, waits for them, and re-layouts  1.41 us (4%)
  between operations  0.64 us (2%)
    pallas_call x1, Pallas kernels, on_device(): pl.pallas_call(functools.partial(kernel, nctx, nch), out_shape=tuple((plt...  32.2 us
    unnamed x2, local copies, waits for them, and re-layouts  1.41 us

profile of v1, /device:TPU:1, one launch (start us, length us, event | category | flops | bytes accessed | tf_op | source)
XLA Modules:
  0.0 34.2 jit_solution(16671300532742254897)
XLA Ops:
  0.6 32.2 %shard_map.140 = (bf16[2,128,512]{2,1,0:T(8,128)(2,1)S(1)}, bf16[4,64,512]{2,1,0:T(8,128)(2,1)S(1)}) custom-call(bf16[2,128,512]{2,1,0:T(8,128)(2,1)} %x_hbm.1, bf16[2,128,512]{2,1,0:T(8,128)(2,1)} %gate_hbm.1, f32[4,512]{1,0:T(4,128)} %cw_hbm.1, f32[512]{0:T(512)} %cb_hbm.1, bf16[288,512]{1,0:T(8,128)(2,1)} %bitcast.1, bf16[256,512]{1,0:T(8,128)(2,1)} %dtw_hbm.1, ...), custom_call_target="tpu_custom_call" | custom-call | tf_op jit(solution)/shard_map/pallas_call | solution.py:537
  32.8 0.7 %copy.17 = bf16[2,128,512]{2,1,0:T(8,128)(2,1)} copy(bf16[2,128,512]{2,1,0:T(8,128)(2,1)S(1)} %get-tuple-element.2) | data formatting | bytes 524288
  33.5 0.7 %copy.18 = bf16[4,64,512]{2,1,0:T(8,128)(2,1)} copy(bf16[4,64,512]{2,1,0:T(8,128)(2,1)S(1)} %get-tuple-element.3) | data formatting | bytes 524288

commit v2 on v1

--- a/solution.py
+++ b/solution.py
@@ -45,7 +45,7 @@
     x_hbm, gate_hbm, cw_hbm, cb_hbm, xw_hbm, dtw_hbm, dtb_hbm, a_hbm, skip_hbm, len_ref, req_hbm, dx_hbm, dg_hbm,
     out_ref, dout_ref,
     x_ref, gate_ref, cw_ref, cb_ref, xw_ref, dtw_ref, dtb_ref, a_ref, skip_ref, req_ref, dx_ref, dg_ref,
-    hw, xe, u_pre, u_dec, edge_u, edge, send_pre, send_dec, rs_pre, rs_dec, ag_pre, ag_dec, wx, a2, skips,
+    hw, xe, u_pre, u_dec, edge_u, edge, send_pre, send_dec, rs_pre, rs_dec, ag_pre, ag_dec, wx, a2, a2b, skips,
     dt_pre, dt_dec, bc_pre, bc_dec, d_all, e_pre, e_dec, ssum, st32, states, hexcl, sexcl, pseg, weight, prefix,
     y_loc, y_nat, y_dec, y_half, y_fin, g_pre, g_dec, mask_dec,
     in_sems, hw_send, hw_recv, ed_send, ed_recv, rsp_send, rsp_recv, rsd_send, rsd_recv,
@@ -72,19 +72,22 @@
     ]
     loads = []
     for i, (src, dst) in enumerate(pairs):
-        if dst.dtype == BF16 and len(dst.shape) == 3:
-            pieces = [(k, pl.ds(j * 32, 32)) for k in range(dst.shape[0]) for j in range(dst.shape[1] // 32)]
-        elif dst.dtype == BF16:
-            pieces = [(pl.ds(j * 32, 32),) for j in range(dst.shape[0] // 32)]
+        sem = in_sems.at[i]
+        if len(dst.shape) == 3:
+            pieces = [(src.at[k], dst.at[k]) for k in range(dst.shape[0])]
         else:
-            pieces = [None]
-        sem = in_sems.at[i]
-        for piece in pieces:
-            if piece is None:
-                pltpu.make_async_copy(src, dst, sem).start()
-            else:
-                pltpu.make_async_copy(src.at[piece], dst.at[piece], sem).start()
-        loads.append(pltpu.make_async_copy(src, dst, sem))
+            pieces = [(src, dst)]
+        if i == 0:
+            half = pl.ds(0, seq // 2), pl.ds(seq // 2, seq // 2)
+            pieces = [(a.at[rows], b.at[rows]) for a, b in pieces for rows in half]
+        loads.append((pltpu.make_async_copy(src, dst, sem), [pltpu.make_async_copy(a, b, sem) for a, b in pieces]))
+
+    def begin(some):
+        for load, pieces in some:
+            for piece in pieces:
+                piece.start()
+
+    begin(loads[:4])
 
     def far_ch():
         for k in sorted(range(1, nch), key=lambda k: -(ring(k // SIDE) + ring(k % SIDE))):
@@ -104,6 +107,8 @@
     for axis in ("ch", "ctx"):
         for k, to in far[axis]():
             pl.semaphore_signal(barrier, inc=1, device_id={axis: to}, device_id_type=MESH)
+
+    begin(loads[4:])
 
     def spread(axis, src, dst, send_sem, recv_sem):
         for k, to in far[axis]():
@@ -134,7 +139,7 @@
         send[:, :, pl.ds(0, rank)] = proj[:, :rank].astype(BF16).reshape(nch, part, rank)
         send[:, :, pl.ds(rank, LANES)] = split(proj[:, rank:]).reshape(nch, part, LANES)
 
-    loads[0].wait()
+    loads[0][0].wait()
     x2 = x_ref[...].reshape(tokens, width)
     q = lax.broadcasted_iota(jnp.int32, (16, tokens), 0)
     col = lax.broadcasted_iota(jnp.int32, (16, tokens), 1)
@@ -154,12 +159,12 @@
     sub = lax.broadcasted_iota(jnp.int32, (SEG, width), 0)
     for r in range(nreq):
         xe[r, pl.ds(3 * SEG, seq), :] = jnp.dot(perm, x_ref[r], preferred_element_type=F32)
-    loads[1].wait()
+    loads[1][0].wait()
     wx[pl.ds(0, rank + 2 * nstate), :] = xw_ref[...]
     wx[pl.ds(rank + 2 * nstate, 2 * nstate), :] = xw_ref[pl.ds(rank, 2 * nstate), :]
     wx[pl.ds(rank + 4 * nstate, LANES - 4 * nstate), :] = jnp.zeros((LANES - 4 * nstate, width), BF16)
-    loads[2].wait()
-    loads[3].wait()
+    loads[2][0].wait()
+    loads[3][0].wait()
     cb = cb_ref[...].reshape(1, width)
     for r in range(nreq):
         for k in range(KCONV - 1):
@@ -170,9 +175,12 @@
     fill(send_pre, project(u_pre[...].astype(BF16)))
     spread("ch", lambda to: send_pre.at[to], lambda k: rs_pre.at[k - 1], rsp_send, rsp_recv)
 
-    for load in loads[4:10]:
+    for load, _ in loads[4:10]:
         load.wait()
     a2[...] = a_ref[...] * (-LOG2E)
+    for c in range(chunks):
+        for n in range(nstate):
+            a2b[c, n] = row_of(a2[n : n + 1, c * LANES : (c + 1) * LANES])
     dtb = dtb_ref[...].reshape(1, width)
     skip = skip_ref[...].reshape(1, width)
     for c in range(chunks):
@@ -240,7 +248,7 @@
         spread("ch", lambda to: ag.at[me_ch], lambda k: ag.at[me_ch], ag_send, ag_recv)
 
     reduce(send_pre, rs_pre, ag_pre, rsp_recv, agp_send, agp_recv)
-    for load in loads[10:]:
+    for load, _ in loads[10:]:
         load.wait()
     for r in range(nreq):
         for c in range(chunks):
@@ -310,8 +318,8 @@
     def lanes_of(c):
         return pl.ds(pl.multiple_of(c * LANES, LANES), LANES)
 
-    def rates(lanes):
-        return [row_of(a2[n : n + 1, lanes]) for n in range(nstate)]
+    def rates(c):
+        return [a2b[c, n] for n in range(nstate)]
 
     def of(n):
         return pl.ds(n * LANES, LANES)
@@ -320,7 +328,7 @@
         def body(c, carry):
             rc = r * chunks + c
             lanes = lanes_of(c)
-            rate = rates(lanes)
+            rate = rates(c)
             h = [None] * nstate
             total = None
             for j in range(nj):
@@ -345,10 +353,10 @@
                 hexcl[rc, n] = jnp.where(sub1 >= 1, pltpu.roll(h[n], 1, 0), 0.0)
             return carry
 
-        lax.fori_loop(0, chunks, body, 0)
-        spread(
-            "ctx", lambda to: states.at[r, me_ctx], lambda k: states.at[r, me_ctx], st_send.at[r], st_recv.at[r]
-        )
+        for first in range(0, chunks, 2):
+            lax.fori_loop(first, first + 2, body, 0)
+            own = states.at[r, me_ctx, pl.ds(first, 2)]
+            spread("ctx", lambda to: own, lambda k: own, st_send.at[r], st_recv.at[r])
 
     for r in range(nreq):
         first_pass(r)
@@ -360,55 +368,33 @@
     dt_dec[...] = step_sizes(proj_dec)
     expand(proj_dec, bc_dec, (0, 1))
 
-    def decode_local(gc, carry):
-        g, c = gc // chunks, gc % chunks
+    def decode_local(c, carry):
         lanes = lanes_of(c)
-        rate = rates(lanes)
+        rate = rates(c)
         skipping = row_of(skips[pl.ds(c, 1), :])
-        h, product = [None] * nstate, [None] * nstate
-        for s in range(steps):
-            rows = pl.ds(pl.multiple_of(s * drows + g * SEG, SEG), SEG)
-            dt = dt_dec[rows, lanes]
-            u = u_dec[rows, lanes]
-            dtu = dt * u
-            terms = [skipping * u]
-            for n in range(nstate):
-                decay = jnp.exp2(dt * rate[n])
-                cout = bc_dec[rows, of(nstate + n)]
-                drive = dtu * bc_dec[rows, of(n)]
-                h[n] = drive if s == 0 else decay * h[n] + drive
-                product[n] = decay if s == 0 else decay * product[n]
-                terms.append(cout * h[n])
-                e_dec[gc, s, n] = cout * product[n]
-            y_dec[rows, lanes] = total_of(terms)
-        return carry
-
-    lax.fori_loop(0, groups * chunks, decode_local, 0)
-
-    def prefill_local(rc, carry):
-        r, c = rc // chunks, rc % chunks
-        lanes = lanes_of(c)
-        skipping = row_of(skips[pl.ds(c, 1), :])
-        h = [hexcl[rc, n] for n in range(nstate)]
-        for n in range(nstate):
-            pseg[rc, n] = jnp.exp2(row_of(a2[n : n + 1, lanes]) * sexcl[rc])
-        product = [None] * nstate
-        for j in range(nj):
-            rows = pl.ds(pl.multiple_of(r * seq + j * SEG, SEG), SEG)
-            u = u_pre[rows, lanes]
-            dtu = dt_pre[rows, lanes] * u
-            terms = [skipping * u]
-            for n in range(nstate):
-                decay = d_all[rc, j, n]
-                cout = bc_pre[rows, of(nstate + n)]
-                h[n] = decay * h[n] + dtu * bc_pre[rows, of(n)]
-                product[n] = decay if j == 0 else decay * product[n]
-                terms.append(cout * h[n])
-                e_pre[rc, j, n] = cout * product[n]
-            y_loc[rc, j] = total_of(terms)
-        return carry
-
-    lax.fori_loop(0, nrc, prefill_local, 0)
+
+        def group(g, carry):
+            h, product = [None] * nstate, [None] * nstate
+            for s in range(steps):
+                rows = pl.ds(pl.multiple_of(s * drows + g * SEG, SEG), SEG)
+                dt = dt_dec[rows, lanes]
+                u = u_dec[rows, lanes]
+                dtu = dt * u
+                terms = [skipping * u]
+                for n in range(nstate):
+                    decay = jnp.exp2(dt * rate[n])
+                    cout = bc_dec[rows, of(nstate + n)]
+                    drive = dtu * bc_dec[rows, of(n)]
+                    h[n] = drive if s == 0 else decay * h[n] + drive
+                    product[n] = decay if s == 0 else decay * product[n]
+                    terms.append(cout * h[n])
+                    e_dec[g * chunks + c, s, n] = cout * product[n]
+                y_dec[rows, lanes] = total_of(terms)
+            return carry
+
+        return lax.fori_loop(0, groups, group, carry, unroll=4)
+
+    lax.fori_loop(0, chunks, decode_local, 0)
 
     all_of(ssum, nctx, ss_recv)
     for rc in range(nrc):
@@ -426,14 +412,28 @@
                 h = weight[rc, i] * h + states[r, i, c].astype(F32)
             prefix[rc, nctx] = h
 
-    def prefill_rest(rc, carry):
-        h = [pseg[rc, n] * row_of(prefix[rc, me_ctx, n : n + 1, :]) for n in range(nstate)]
+    def prefill_states(rc, carry):
+        r, c = rc // chunks, rc % chunks
+        lanes = lanes_of(c)
+        skipping = row_of(skips[pl.ds(c, 1), :])
+        start = sexcl[rc]
+        h = [
+            hexcl[rc, n]
+            + jnp.exp2(a2b[c, n] * start) * row_of(prefix[rc, me_ctx, n : n + 1, :])
+            for n in range(nstate)
+        ]
         for j in range(nj):
-            y = total_of([y_loc[rc, j]] + [e_pre[rc, j, n] * h[n] for n in range(nstate)])
-            y_nat[rc, pl.ds(j, SEG, stride=nj), :] = y
+            rows = pl.ds(pl.multiple_of(r * seq + j * SEG, SEG), SEG)
+            u = u_pre[rows, lanes]
+            dtu = dt_pre[rows, lanes] * u
+            terms = [skipping * u]
+            for n in range(nstate):
+                h[n] = d_all[rc, j, n] * h[n] + dtu * bc_pre[rows, of(n)]
+                terms.append(bc_pre[rows, of(nstate + n)] * h[n])
+            y_nat[rc, pl.ds(j, SEG, stride=nj), :] = total_of(terms)
         return carry
 
-    lax.fori_loop(0, nrc, prefill_rest, 0)
+    lax.fori_loop(0, nrc, prefill_states, 0)
 
     def decode_rest(c, carry):
         lanes = lanes_of(c)
@@ -507,6 +507,7 @@
         pltpu.VMEM((nch, dpart, cols), BF16),
         pltpu.VMEM((cols, width), BF16),
         pltpu.VMEM((nstate, width), F32),
+        pltpu.VMEM((chunks, nstate, SEG, LANES), F32),
         pltpu.VMEM((8, LANES), F32),
         pltpu.VMEM((tokens, width), F32),
         pltpu.VMEM((dtokens, width), F32),

time: 34.4 us -> 33 us (0.959)
  Pallas kernels: 32.2 us -> 30.8 us
    pallas_call x1, Pallas kernels: 32.2 us -> 30.8 us  [on_device(): pl.pallas_call(functools.partial(kernel, nctx, nch), out_shape=tuple((plt...]
where the time goes in v2:
time: 33 us; the launch traced here: 32.8 us
  Pallas kernels  30.8 us (93%)
  local copies, waits for them, and re-layouts  1.41 us (4%)
  between operations  0.64 us (2%)
    pallas_call x1, Pallas kernels, on_device(): pl.pallas_call(functools.partial(kernel, nctx, nch), out_shape=tuple((plt...  30.8 us
    unnamed x2, local copies, waits for them, and re-layouts  1.41 us

profile of v2, /device:TPU:1, one launch (start us, length us, event | category | flops | bytes accessed | tf_op | source)
XLA Modules:
  0.0 32.8 jit_solution(10076732882894620590)
XLA Ops:
  0.6 30.8 %shard_map.140 = (bf16[2,128,512]{2,1,0:T(8,128)(2,1)S(1)}, bf16[4,64,512]{2,1,0:T(8,128)(2,1)S(1)}) custom-call(bf16[2,128,512]{2,1,0:T(8,128)(2,1)} %x_hbm.1, bf16[2,128,512]{2,1,0:T(8,128)(2,1)} %gate_hbm.1, f32[4,512]{1,0:T(4,128)} %cw_hbm.1, f32[512]{0:T(512)} %cb_hbm.1, bf16[288,512]{1,0:T(8,128)(2,1)} %bitcast.1, bf16[256,512]{1,0:T(8,128)(2,1)} %dtw_hbm.1, ...), custom_call_target="tpu_custom_call" | custom-call | tf_op jit(solution)/shard_map/pallas_call | solution.py:538
  31.4 0.7 %copy.17 = bf16[2,128,512]{2,1,0:T(8,128)(2,1)} copy(bf16[2,128,512]{2,1,0:T(8,128)(2,1)S(1)} %get-tuple-element.2) | data formatting | bytes 524288
  32.1 0.7 %copy.18 = bf16[4,64,512]{2,1,0:T(8,128)(2,1)} copy(bf16[4,64,512]{2,1,0:T(8,128)(2,1)S(1)} %get-tuple-element.3) | data formatting | bytes 524288

commit v3 on v2

--- a/solution.py
+++ b/solution.py
@@ -19,7 +19,7 @@
 
 
 def softplus(x):
-    return jnp.maximum(x, 0.0) + jnp.log1p(jnp.exp(-jnp.abs(x)))
+    return jnp.maximum(x, 0.0) + jnp.log(1.0 + jnp.exp(-jnp.abs(x)))
 
 
 def silu(x):
@@ -44,10 +44,10 @@
     nctx, nch,
     x_hbm, gate_hbm, cw_hbm, cb_hbm, xw_hbm, dtw_hbm, dtb_hbm, a_hbm, skip_hbm, len_ref, req_hbm, dx_hbm, dg_hbm,
     out_ref, dout_ref,
-    x_ref, gate_ref, cw_ref, cb_ref, xw_ref, dtw_ref, dtb_ref, a_ref, skip_ref, req_ref, dx_ref, dg_ref,
+    x_ref, gate_ref, cw_ref, cb_ref, dtw_ref, dtb_ref, a_ref, skip_ref, req_ref, dx_ref, dg_ref,
     hw, xe, u_pre, u_dec, edge_u, edge, send_pre, send_dec, rs_pre, rs_dec, ag_pre, ag_dec, wx, a2, a2b, skips,
     dt_pre, dt_dec, bc_pre, bc_dec, d_all, e_pre, e_dec, ssum, st32, states, hexcl, sexcl, pseg, weight, prefix,
-    y_loc, y_nat, y_dec, y_half, y_fin, g_pre, g_dec, mask_dec,
+    y_loc, y_nat, y_dec, y_half, g_pre, g_dec, mask_dec,
     in_sems, hw_send, hw_recv, ed_send, ed_recv, rsp_send, rsp_recv, rsd_send, rsd_recv,
     agp_send, agp_recv, agd_send, agd_recv, ss_send, ss_recv, st_send, st_recv,
 ):
@@ -66,7 +66,7 @@
     offset = me_ctx * seq
 
     pairs = [
-        (x_hbm, x_ref), (xw_hbm, xw_ref), (cw_hbm, cw_ref), (cb_hbm, cb_ref), (dx_hbm, dx_ref), (req_hbm, req_ref),
+        (x_hbm, x_ref), (xw_hbm, wx.at[pl.ds(0, rank + 2 * nstate)]), (cw_hbm, cw_ref), (cb_hbm, cb_ref), (dx_hbm, dx_ref), (req_hbm, req_ref),
         (dtw_hbm, dtw_ref), (dtb_hbm, dtb_ref), (a_hbm, a_ref), (skip_hbm, skip_ref), (gate_hbm, gate_ref),
         (dg_hbm, dg_ref),
     ]
@@ -87,7 +87,12 @@
             for piece in pieces:
                 piece.start()
 
-    begin(loads[:4])
+    begin(loads[:2])
+    twin = pltpu.make_async_copy(
+        xw_hbm.at[pl.ds(rank, 2 * nstate)], wx.at[pl.ds(rank + 2 * nstate, 2 * nstate)], in_sems.at[len(pairs)]
+    )
+    twin.start()
+    begin(loads[2:4])
 
     def far_ch():
         for k in sorted(range(1, nch), key=lambda k: -(ring(k // SIDE) + ring(k % SIDE))):
@@ -160,8 +165,7 @@
     for r in range(nreq):
         xe[r, pl.ds(3 * SEG, seq), :] = jnp.dot(perm, x_ref[r], preferred_element_type=F32)
     loads[1][0].wait()
-    wx[pl.ds(0, rank + 2 * nstate), :] = xw_ref[...]
-    wx[pl.ds(rank + 2 * nstate, 2 * nstate), :] = xw_ref[pl.ds(rank, 2 * nstate), :]
+    twin.wait()
     wx[pl.ds(rank + 4 * nstate, LANES - 4 * nstate), :] = jnp.zeros((LANES - 4 * nstate, width), BF16)
     loads[2][0].wait()
     loads[3][0].wait()
@@ -193,6 +197,19 @@
     edge_u[...] = jnp.zeros_like(edge_u)
 
     all_of(hw, nctx, hw_recv)
+    window = total_of([hw[i].astype(F32) for i in range(nctx)])
+    chosen = jnp.broadcast_to(request, (drows, width)) > 0.5
+    recent = [
+        jnp.where(chosen, row_of(window[9 + k : 10 + k], drows), row_of(window[6 + k : 7 + k], drows))
+        for k in range(KCONV - 1)
+    ]
+    recent = recent + [dx_ref[s].astype(F32) for s in range(steps)]
+    for s in range(steps):
+        conv = cb + sum(cw_ref[k : k + 1] * recent[s + k] for k in range(KCONV))
+        u_dec[pl.ds(s * drows, drows), :] = silu(conv).astype(BF16).astype(F32)
+    fill(send_dec, project(u_dec[...].astype(BF16)))
+    spread("ch", lambda to: send_dec.at[to], lambda k: rs_dec.at[k - 1], rsd_send, rsd_recv)
+
     before = hw[lax.rem(me_ctx + nctx - 1, nctx)].astype(F32)
     before = jnp.where(me_ctx > 0, before, 0.0)
     edges = KCONV - 1
@@ -220,19 +237,6 @@
     packed = jnp.where(spot < count, edge_proj[:, :LANES], jnp.where(spot < 2 * count, lower, packed))
     edge[me_ch] = packed.astype(BF16)
     spread("ch", lambda to: edge.at[me_ch], lambda k: edge.at[me_ch], ed_send, ed_recv)
-
-    window = total_of([hw[i].astype(F32) for i in range(nctx)])
-    chosen = jnp.broadcast_to(request, (drows, width)) > 0.5
-    recent = [
-        jnp.where(chosen, row_of(window[9 + k : 10 + k], drows), row_of(window[6 + k : 7 + k], drows))
-        for k in range(KCONV - 1)
-    ]
-    recent = recent + [dx_ref[s].astype(F32) for s in range(steps)]
-    for s in range(steps):
-        conv = cb + sum(cw_ref[k : k + 1] * recent[s + k] for k in range(KCONV))
-        u_dec[pl.ds(s * drows, drows), :] = silu(conv).astype(BF16).astype(F32)
-    fill(send_dec, project(u_dec[...].astype(BF16)))
-    spread("ch", lambda to: send_dec.at[to], lambda k: rs_dec.at[k - 1], rsd_send, rsd_recv)
 
     def summed(terms):
         total = total_of(terms)
@@ -392,7 +396,7 @@
                 y_dec[rows, lanes] = total_of(terms)
             return carry
 
-        return lax.fori_loop(0, groups, group, carry, unroll=4)
+        return lax.fori_loop(0, groups, group, carry, unroll=8)
 
     lax.fori_loop(0, chunks, decode_local, 0)
 
@@ -442,16 +446,22 @@
             at = range(first, first + half)
             f0 = [row_of(prefix[c, nctx, n : n + 1, :]) for n in at]
             f1 = [row_of(prefix[chunks + c, nctx, n : n + 1, :]) for n in at]
-            for g in range(groups):
-                mine = mask_dec[g * SEG : (g + 1) * SEG, :] > 0.5
-                h = [jnp.where(mine, b, a) for a, b in zip(f0, f1)]
-                for s in range(steps):
-                    rows = pl.ds(s * drows + g * SEG, SEG)
-                    terms = [e_dec[g * chunks + c, s, n] * h[n - first] for n in at]
-                    if first == 0:
-                        y_half[rows, lanes] = total_of(terms + [y_dec[rows, lanes]])
-                    else:
-                        y_fin[rows, lanes] = total_of(terms + [y_half[rows, lanes]]) * g_dec[rows, lanes]
+            for g in range(0, groups, 2):
+                pair = []
+                for k in (g, g + 1):
+                    mine = mask_dec[k * SEG : (k + 1) * SEG, :] > 0.5
+                    h = [jnp.where(mine, b, a) for a, b in zip(f0, f1)]
+                    done = []
+                    for s in range(steps):
+                        rows = pl.ds(s * drows + k * SEG, SEG)
+                        terms = [e_dec[k * chunks + c, s, n] * h[n - first] for n in at]
+                        if first == 0:
+                            y_half[rows, lanes] = total_of(terms + [y_dec[rows, lanes]])
+                        else:
+                            done.append(total_of(terms + [y_half[rows, lanes]]) * g_dec[rows, lanes])
+                    pair.append(done)
+                for s, (a, b) in enumerate(zip(*pair)):
+                    dout_ref[s, pl.ds(g * SEG, 2 * SEG), lanes] = jnp.concatenate([a, b], axis=0).astype(BF16)
         return carry
 
     lax.fori_loop(0, chunks, decode_rest, 0)
@@ -462,8 +472,6 @@
         for c in range(chunks):
             y = y_nat[r * chunks + c] * g_pre[r * chunks + c]
             out_ref[r, :, pl.ds(c * LANES, LANES)] = jnp.where(live, y, 0.0).astype(BF16)
-    for s in range(steps):
-        dout_ref[s] = y_fin[pl.ds(s * drows, drows), :].astype(BF16)
 
     all_of(hw, nctx, hw_send)
     all_of(edge, nch, ed_send)
@@ -492,7 +500,7 @@
     vmem = pl.BlockSpec(memory_space=pltpu.VMEM)
     smem = pl.BlockSpec(memory_space=pltpu.SMEM)
     sem = pltpu.SemaphoreType.DMA
-    scratch = [pltpu.VMEM(a.shape, a.dtype) for i, a in enumerate(args) if i != 9] + [
+    scratch = [pltpu.VMEM(a.shape, a.dtype) for i, a in enumerate(args) if i not in (4, 9)] + [
         pltpu.VMEM((nctx, 16, width), BF16),
         pltpu.VMEM((nreq, (nj + KCONV - 1) * SEG, width), F32),
         pltpu.VMEM((tokens, width), F32),
@@ -528,11 +536,10 @@
         pltpu.VMEM((nrc, seq, LANES), F32),
         pltpu.VMEM((dtokens, width), F32),
         pltpu.VMEM((dtokens, width), F32),
-        pltpu.VMEM((dtokens, width), F32),
         pltpu.VMEM((nrc, seq, LANES), F32),
         pltpu.VMEM((dtokens, width), F32),
         pltpu.VMEM((drows, LANES), F32),
-        sem((len(args) - 1,)),
+        sem((len(args),)),
     ] + [sem] * 14 + [sem((nreq,))] * 2
     shapes = (jax.ShapeDtypeStruct(inputs.shape, BF16), jax.ShapeDtypeStruct(dec_inputs.shape, BF16))
     return pl.pallas_call(

time: 33 us -> 32.4 us (0.982)
  Pallas kernels: 30.8 us -> 30.2 us
    pallas_call x1, Pallas kernels: 30.8 us -> 30.2 us  [on_device(): pl.pallas_call(functools.partial(kernel, nctx, nch), out_shape=tuple((plt...]
where the time goes in v3:
time: 32.4 us; the launch traced here: 32.2 us
  Pallas kernels  30.2 us (93%)
  local copies, waits for them, and re-layouts  1.41 us (4%)
  between operations  0.64 us (2%)
    pallas_call x1, Pallas kernels, on_device(): pl.pallas_call(functools.partial(kernel, nctx, nch), out_shape=tuple((plt...  30.2 us
    unnamed x2, local copies, waits for them, and re-layouts  1.41 us

profile of v3, /device:TPU:1, one launch (start us, length us, event | category | flops | bytes accessed | tf_op | source)
XLA Modules:
  0.0 32.2 jit_solution(2260388823205727619)
XLA Ops:
  0.6 30.2 %shard_map.140 = (bf16[2,128,512]{2,1,0:T(8,128)(2,1)S(1)}, bf16[4,64,512]{2,1,0:T(8,128)(2,1)S(1)}) custom-call(bf16[2,128,512]{2,1,0:T(8,128)(2,1)} %x_hbm.1, bf16[2,128,512]{2,1,0:T(8,128)(2,1)} %gate_hbm.1, f32[4,512]{1,0:T(4,128)} %cw_hbm.1, f32[512]{0:T(512)} %cb_hbm.1, bf16[288,512]{1,0:T(8,128)(2,1)} %bitcast.1, bf16[256,512]{1,0:T(8,128)(2,1)} %dtw_hbm.1, ...), custom_call_target="tpu_custom_call" | custom-call | tf_op jit(solution)/shard_map/pallas_call | solution.py:545
  30.8 0.7 %copy.17 = bf16[2,128,512]{2,1,0:T(8,128)(2,1)} copy(bf16[2,128,512]{2,1,0:T(8,128)(2,1)S(1)} %get-tuple-element.2) | data formatting | bytes 524288
  31.5 0.7 %copy.18 = bf16[4,64,512]{2,1,0:T(8,128)(2,1)} copy(bf16[4,64,512]{2,1,0:T(8,128)(2,1)S(1)} %get-tuple-element.3) | data formatting | bytes 524288

commit v4 on v3

--- a/solution.py
+++ b/solution.py
@@ -196,6 +196,15 @@
     mask_dec[...] = jnp.broadcast_to(request, (drows, LANES))
     edge_u[...] = jnp.zeros_like(edge_u)
 
+    for s in range(steps):
+        rows = pl.ds(s * drows, drows)
+        known = cb + sum(
+            cw_ref[k : k + 1] * dx_ref[s + k - KCONV + 1].astype(F32) for k in range(max(KCONV - 1 - s, 0), KCONV)
+        )
+        if s < KCONV - 1:
+            y_dec[rows, :] = known
+        else:
+            u_dec[rows, :] = silu(known).astype(BF16).astype(F32)
     all_of(hw, nctx, hw_recv)
     window = total_of([hw[i].astype(F32) for i in range(nctx)])
     chosen = jnp.broadcast_to(request, (drows, width)) > 0.5
@@ -203,10 +212,10 @@
         jnp.where(chosen, row_of(window[9 + k : 10 + k], drows), row_of(window[6 + k : 7 + k], drows))
         for k in range(KCONV - 1)
     ]
-    recent = recent + [dx_ref[s].astype(F32) for s in range(steps)]
-    for s in range(steps):
-        conv = cb + sum(cw_ref[k : k + 1] * recent[s + k] for k in range(KCONV))
-        u_dec[pl.ds(s * drows, drows), :] = silu(conv).astype(BF16).astype(F32)
+    for s in range(KCONV - 1):
+        rows = pl.ds(s * drows, drows)
+        conv = y_dec[rows, :] + sum(cw_ref[k : k + 1] * recent[s + k] for k in range(KCONV - 1 - s))
+        u_dec[rows, :] = silu(conv).astype(BF16).astype(F32)
     fill(send_dec, project(u_dec[...].astype(BF16)))
     spread("ch", lambda to: send_dec.at[to], lambda k: rs_dec.at[k - 1], rsd_send, rsd_recv)
 

time: 32.4 us -> 32.3 us (level)
  no operation moved by 1% of the time
where the time goes in v4:
time: 32.3 us; the launch traced here: 32.1 us
  Pallas kernels  30.1 us (93%)
  local copies, waits for them, and re-layouts  1.41 us (4%)
  between operations  0.64 us (2%)
    pallas_call x1, Pallas kernels, on_device(): pl.pallas_call(functools.partial(kernel, nctx, nch), out_shape=tuple((plt...  30.1 us
    unnamed x2, local copies, waits for them, and re-layouts  1.41 us

profile of v4, /device:TPU:1, one launch (start us, length us, event | category | flops | bytes accessed | tf_op | source)
XLA Modules:
  0.0 32.1 jit_solution(9316335834778279259)
XLA Ops:
  0.6 30.1 %shard_map.140 = (bf16[2,128,512]{2,1,0:T(8,128)(2,1)S(1)}, bf16[4,64,512]{2,1,0:T(8,128)(2,1)S(1)}) custom-call(bf16[2,128,512]{2,1,0:T(8,128)(2,1)} %x_hbm.1, bf16[2,128,512]{2,1,0:T(8,128)(2,1)} %gate_hbm.1, f32[4,512]{1,0:T(4,128)} %cw_hbm.1, f32[512]{0:T(512)} %cb_hbm.1, bf16[288,512]{1,0:T(8,128)(2,1)} %bitcast.1, bf16[256,512]{1,0:T(8,128)(2,1)} %dtw_hbm.1, ...), custom_call_target="tpu_custom_call" | custom-call | tf_op jit(solution)/shard_map/pallas_call | solution.py:554
  30.7 0.7 %copy.17 = bf16[2,128,512]{2,1,0:T(8,128)(2,1)} copy(bf16[2,128,512]{2,1,0:T(8,128)(2,1)S(1)} %get-tuple-element.2) | data formatting | bytes 524288
  31.4 0.7 %copy.18 = bf16[4,64,512]{2,1,0:T(8,128)(2,1)} copy(bf16[4,64,512]{2,1,0:T(8,128)(2,1)S(1)} %get-tuple-element.3) | data formatting | bytes 524288
